TPU v7x, 128 devices: a whole 4x4x4 slice. The times are simulated.
128 devices in a mesh: wide: 16 (over x, z), narrow: 8 (over y, core).
Axes of the slice: x: 4, y: 4, z: 4, core: 2. Of those that a mesh axis runs over, the one named last changes fastest.
Arguments:
- tokens: bfloat16 [16384, 2048], P(('wide', 'narrow')), may hold values from -6 to 6
- lengths: int32 [16, 2], P('wide'), may hold values from 1 to 960, 1024 in all within a row
- picks: int32 [16384, 2], P(('wide', 'narrow')), may hold values from 0 to 3
- cotangent: bfloat16 [16384, 2048], P(('wide', 'narrow'))
- block_master: float32 [2048, 24576], P(('wide', 'narrow'))
- block_first: float32 [2048, 24576], P(('wide', 'narrow')), may hold values from -0.00024414062 to 0.00024414062
- block_second: float32 [2048, 24576], P(('wide', 'narrow')), may hold values from 5.111863e-10 to 8.257626e-09
- gains: float32 [2, 2048], replicated
- gains_first: float32 [2, 2048], replicated, may hold values from -0.00048828125 to 0.00048828125
- gains_second: float32 [2, 2048], replicated, may hold values from 4.915253e-09 to 1.9661012e-08
- router_in: float32 [2048, 256], replicated, may hold values from -0.125 to 0.125
- router_in_first: float32 [2048, 256], replicated, may hold values from -0.00024414062 to 0.00024414062
- router_in_second: float32 [2048, 256], replicated, may hold values from 5.111863e-10 to 8.257626e-09
- router_out: float32 [256, 8], replicated, may hold values from -0.27 to 0.27
- router_out_first: float32 [256, 8], replicated, may hold values from -0.00024414062 to 0.00024414062
- router_out_second: float32 [256, 8], replicated, may hold values from 5.111863e-10 to 8.257626e-09
Outputs:
- output: bfloat16 [16384, 2048], P(('wide', 'narrow'))
- input_grad: float32 [16384, 2048], P(('wide', 'narrow'))
- counts: float32 [2, 4], replicated
- grad_norm: float32 [], replicated
- new_block: float32 [2048, 24576], P(('wide', 'narrow'))
- new_block_first: float32 [2048, 24576], P(('wide', 'narrow'))
- new_block_second: float32 [2048, 24576], P(('wide', 'narrow'))
- block_copy: bfloat16 [2048, 24576], P(('wide', 'narrow'))
- new_gains: float32 [2, 2048], replicated
- new_gains_first: float32 [2, 2048], replicated
- new_gains_second: float32 [2, 2048], replicated
- new_router_in: float32 [2048, 256], replicated
- new_router_in_first: float32 [2048, 256], replicated
- new_router_in_second: float32 [2048, 256], replicated
- new_router_out: float32 [256, 8], replicated
- new_router_out_first: float32 [256, 8], replicated
- new_router_out_second: float32 [256, 8], replicated
Inputs may be any that keep to these rules, and one draw needn't show every extreme that they name: `lengths`: each row sums to 1024.
All inputs are finite; a program needn't handle non-finite values.
Results may differ from a plain program's by a relative error of at most 0.023.
Values may be sent and summed in bfloat16 or wider, within the bound.
A program may use at most 640 MiB of HBM per device.

v0:
```python
import functools

import jax
import jax.numpy as jnp
import numpy as np
from jax import lax
from jax.experimental import pallas as pl
from jax.experimental.pallas import tpu as pltpu
from jax.sharding import PartitionSpec as P

D = 2048
HEADS = 16
HEAD_DIM = 128
FF = 8192
RH = 256
LEVELS = 4
STEP = 10
TOK = 128
GROUP = 1024
SIDE = 4
WIDE = 16
NARROW = 8
ROWS = 16

VECTOR_ROWS = 64
GAIN_ROWS = 2 * D // 128
SMALL_ROWS = GAIN_ROWS + RH * 2 * LEVELS // 128
SQUARE_ROWS = 8

NORM_EPS = 1e-05
CLIP_NORM = 1.0
CONTRACT_COLS = (((1,), (1,)), ((), ()))
CONTRACT_ROWS = (((0,), (0,)), ((), ()))
MESH = pl.DeviceIdType.MESH
BF = jnp.bfloat16
F32 = jnp.float32


(
    CA, DA, DOWN, DS, FEED, FIRST, GATES, GATHER, GD, GE, GG, GM, GO, GQ, GU, GX, HID, L1, LB,
    LD, LN, MIXED, MO, MORE, N0, N1, N2, N3, OUT, P0, P1, P2, P3, Q, RF, RT, SA, SD, SL, SQ, SU,
    T0, T1, T2, T3, TB, TOTAL, U0, U1, U2, U3, UP, V0, V1, V2, V3, WA, WD, WU, Y0, Y1, Y2, Y3,
) = range(63)
ATTEND = (T0, T1, T2, T3)
EARLY = (V0, V1, V2, V3)
UNITS = (U0, U1, U2, U3)
OUTPUT = (Y0, Y1, Y2, Y3)
NORM = (N0, N1, N2, N3)
PAIR = (P0, P1, P2, P3)


FORWARD_PLAN = (
    CA, SA, L1, SU, RF, GM, SD, GM, SA, WA, GM, GX, WA, SU, GX, WA, GM, GM, WA, GX, WA, SD, GG,
    SL, WA, WU, GX, WD, GX, GM, GX, WU, WA, TB, GG, Q, WD, GM, GG, T2, T1, WD, TOTAL, T3, T0,
    TOTAL, WD, TOTAL, WD, GX, GG, SL, GG, WD, WU, TOTAL, WU, WU, WD, GG, DA, WU, GG, TOTAL,
    TOTAL, LN, WU, TOTAL, WU, GG,
)
FEED_PLAN = (
    GATHER, WU, WU, GATHER, WU, LD, GATHER, WU, WU, V0, WU, GATHER, V1, WU, V3, U1, GATHER, U3,
    N1, N3, GATHER, V2, U2, TOTAL, TOTAL, N2, U0, GE, TOTAL, DS, Y2, MORE, GD, FIRST, N0,
    GATHER, TOTAL, GU, FIRST, TOTAL, MORE, TOTAL, TOTAL, LB, HID, Y3, Y1, Y0, HID, FIRST, FIRST,
    MORE, HID,
)
BACKWARD_PLAN = (
    GATHER, UP, LD, GATES, UP, GATHER, GATHER, DOWN, FEED, P0, FEED, GATHER, P3, GATHER, P1,
    FEED, GATHER, DOWN, GATES, UP, P2, DOWN, GATHER, GO, MO, FEED, UP, GATES, RT, N2, GATES, N1,
    MO, GQ, UP, MIXED, GATES, TOTAL, MO, TOTAL, MIXED, DOWN, N3, N0, TOTAL, MO, GATES, TOTAL,
    FEED, MIXED, GATES, FEED, MIXED, TOTAL, GATES, MO, MIXED, TOTAL, GATES, GATES, MO, DOWN,
    TOTAL, MO, LB, UP, OUT, SQ, MIXED, UP,
)


def here():
    w = lax.axis_index("wide")
    n = lax.axis_index("narrow")
    return lax.div(w, SIDE), lax.rem(w, SIDE), lax.div(n, 2), lax.rem(n, 2)


def wrap(i):
    return lax.rem(i + 2 * SIDE, SIDE)


def moved(dx=0, dz=0, dy=0, dc=0):
    x, z, y, c = here()
    return (wrap(x + dx) * SIDE + wrap(z + dz), wrap(y + dy) * 2 + lax.rem(c + dc, 2))


NEAR_Y = [dict(dy=1), dict(dy=-1), dict(dc=1)]
NARROW_ALL = [dict(dy=a, dc=b) for a in range(SIDE) for b in range(2) if a or b]
NEAR_XZ = [dict(dx=1), dict(dx=-1), dict(dz=1), dict(dz=-1)]
LINES_XZ = [dict(dx=a) for a in (1, 2, 3)] + [dict(dz=a) for a in (1, 2, 3)]
WIDE_ALL = [dict(dx=a, dz=b) for a in range(SIDE) for b in range(SIDE) if a or b]


def greet(partners):
    barrier = pltpu.get_barrier_semaphore()
    for p in partners:
        pl.semaphore_signal(barrier, inc=1, device_id=moved(**p), device_id_type=MESH)
    pl.semaphore_wait(barrier, len(partners))


def span(start, size):
    if not isinstance(start, int):
        start = pl.multiple_of(start, ROWS)
    return pl.ds(start, size)


def lanes(start, size):
    if not isinstance(start, int):
        start = pl.multiple_of(start, 128)
    return pl.ds(start, size)


def step(*parts):
    for part in parts:
        next(part, None)


class Net:
    def __init__(self, send, recv, local):
        self.send, self.recv, self.local = send, recv, local
        self.used, self.used_local = 0, 0
        self.sent = []

    def put(self, src, dst, target):
        i = self.used
        self.used += 1
        copy = pltpu.make_async_remote_copy(
            src_ref=src,
            dst_ref=dst,
            send_sem=self.send.at[i],
            recv_sem=self.recv.at[i],
            device_id=target,
            device_id_type=MESH,
        )
        copy.start()
        self.sent.append(copy)
        return copy

    def keep(self, src, dst):
        i = self.used_local
        self.used_local += 1
        copy = pltpu.make_async_copy(src, dst, self.local.at[i])
        copy.start()
        return copy

    def sent_by(self, *copies):
        for copy in copies:
            copy.wait_send()
        done = [id(copy) for copy in copies]
        self.sent = [copy for copy in self.sent if id(copy) not in done]

    def finish(self):
        for copy in self.sent:
            copy.wait_send()


def take_turns(*parts):
    live = list(parts)
    while live:
        still = []
        for part in live:
            try:
                next(part)
                still.append(part)
            except StopIteration:
                pass
        live = still


def follow(plan, works, moves):
    for name in plan:
        if name in works:
            works[name]()
        else:
            next(moves[name], None)
    take_turns(*moves.values())


def comm_call(body, ins, outs, scratch, cid, copies, locals_, name, vmem=63, cost=None):
    n_in, n_out, n_scr = len(ins), len(outs), len(scratch)

    def kernel(*refs):
        in_refs = refs[:n_in]
        out_refs = refs[n_in : n_in + n_out]
        scr = refs[n_in + n_out : n_in + n_out + n_scr]
        send, recv, local = refs[n_in + n_out + n_scr :]
        net = Net(send, recv, local)
        body(net, in_refs, out_refs, scr)
        net.finish()
        assert net.used <= copies and net.used_local <= locals_, (net.used, net.used_local)

    return pl.pallas_call(
        kernel,
        out_shape=outs,
        in_specs=[pl.BlockSpec(memory_space=pl.ANY)] * n_in,
        out_specs=[pl.BlockSpec(memory_space=pl.ANY)] * n_out,
        scratch_shapes=list(scratch)
        + [
            pltpu.SemaphoreType.DMA((copies,)),
            pltpu.SemaphoreType.DMA((copies,)),
            pltpu.SemaphoreType.DMA((max(locals_, 1),)),
        ],
        compiler_params=pltpu.CompilerParams(
            collective_id=cid, has_side_effects=True, vmem_limit_bytes=vmem * 2**20
        ),
        name=name,
        cost_estimate=cost,
    )(*ins)


def gather_narrow(net, own, out):
    x, z, y, c = here()
    rows = own.shape[0]
    half = rows // 2

    def block(dy, lo=0, size=rows):
        return out.at[span((wrap(y + dy) * 2 + c) * rows + lo, size)]

    first, last = own.at[pl.ds(0, half)], own.at[pl.ds(half, half)]
    up = net.put(first, block(0, 0, half), moved(dy=1))
    down = net.put(last, block(0, half, half), moved(dy=-1))
    up_late = net.put(last, block(0, half, half), moved(dy=1))
    down_late = net.put(first, block(0, 0, half), moved(dy=-1))
    across = [net.put(own, block(0), moved(dc=1))]
    mine = net.keep(own, block(0))
    yield
    mine.wait()
    across[0].wait_recv()
    yield
    up.wait_recv()
    on = net.put(block(-1, 0, half), block(-1, 0, half), moved(dy=1))
    down.wait_recv()
    back = net.put(block(1, half, half), block(1, half, half), moved(dy=-1))
    yield
    up_late.wait_recv()
    across.append(net.put(block(-1), block(-1), moved(dc=1)))
    down_late.wait_recv()
    across.append(net.put(block(1), block(1), moved(dc=1)))
    across[1].wait_recv()
    across[2].wait_recv()
    yield
    on.wait_recv()
    across.append(net.put(block(2, 0, half), block(2, 0, half), moved(dc=1)))
    back.wait_recv()
    across.append(net.put(block(2, half, half), block(2, half, half), moved(dc=1)))
    yield
    across[3].wait_recv()
    across[4].wait_recv()
    yield
    net.sent_by(up, down, up_late, down_late, on, back, *across)


GATHER_COPIES = 12


def gather_small(net, own, out):
    c = here()[3]
    y = here()[2]
    rows = own.shape[0]

    def block(dy):
        return out.at[span((wrap(y + dy) * 2 + c) * rows, rows)]

    along = [net.put(own, block(0), moved(dy=d)) for d in (2, 1, 3)]
    across = [net.put(own, block(0), moved(dc=1))]
    mine = net.keep(own, block(0))
    yield
    for copy, d in zip(along, (2, 1, 3)):
        copy.wait_recv()
        across.append(net.put(block(-d), block(-d), moved(dc=1)))
    yield
    mine.wait()
    for copy in across:
        copy.wait_recv()


GATHER_SMALL_COPIES = 7


def gather_call(own, cid, name):
    rows, cols = own.shape

    def body(net, ins, outs, scr):
        greet(NEAR_Y)
        take_turns(gather_narrow(net, ins[0], outs[0]))

    return comm_call(
        body,
        [own],
        [jax.ShapeDtypeStruct((NARROW * rows, cols), own.dtype)],
        [],
        cid,
        GATHER_COPIES,
        1,
        name,
    )[0]


def reduce_scratch(rows, cols):
    return [
        pltpu.VMEM((SIDE, rows, cols), BF),
        pltpu.VMEM((SIDE, rows, cols), BF),
        pltpu.VMEM((2, rows // 2, cols), BF),
        pltpu.VMEM((2, rows, cols), BF),
        pltpu.VMEM((3, rows, cols), BF),
        pltpu.VMEM((rows, cols), F32),
    ]


REDUCE_COPIES = 10
REDUCE_LOCALS = 5


def reduce_narrow(net, part, scr):
    own, other, through, landed, ready, total = scr
    x, z, y, c = here()
    rows, cols = total.shape
    half = rows // 2

    def block(dy, core):
        return part.at[span((wrap(y + dy) * 2 + core) * rows, rows)]

    order = (2, 1, 3, 0)
    local, cross = {}, {}
    for dy in order:
        cross[dy] = net.put(block(dy, 1 - c), other.at[dy], moved(dc=1))
        local[dy] = net.keep(block(dy, c), own.at[dy])

    def pair(dy, lo, size):
        s = span(lo, size)
        return own[dy, s, :].astype(F32) + other[dy, s, :].astype(F32)

    yield
    local[2].wait()
    cross[2].wait_recv()
    ready[0] = pair(2, 0, rows).astype(BF)
    first, last = span(0, half), span(half, half)
    via_up = net.put(ready.at[0, first], through.at[0], moved(dy=1))
    via_down = net.put(ready.at[0, last], through.at[1], moved(dy=-1))
    yield
    local[1].wait()
    cross[1].wait_recv()
    ready[1, last, :] = pair(1, half, half).astype(BF)
    up_late = net.put(ready.at[1, last], landed.at[0, last], moved(dy=1))
    local[3].wait()
    cross[3].wait_recv()
    ready[2, first, :] = pair(3, 0, half).astype(BF)
    down_first = net.put(ready.at[2, first], landed.at[1, first], moved(dy=-1))
    yield
    via_up.wait_recv()
    ready[1, first, :] = (pair(1, 0, half) + through[0].astype(F32)).astype(BF)
    up_first = net.put(ready.at[1, first], landed.at[0, first], moved(dy=1))
    via_down.wait_recv()
    ready[2, last, :] = (pair(3, half, half) + through[1].astype(F32)).astype(BF)
    down_late = net.put(ready.at[2, last], landed.at[1, last], moved(dy=-1))
    yield
    local[0].wait()
    cross[0].wait_recv()
    total[...] = pair(0, 0, rows)
    yield
    for copy in (up_late, down_first, up_first, down_late):
        copy.wait_recv()
    total[...] += landed[0].astype(F32) + landed[1].astype(F32)


def pairs_scratch(rows, cols):
    return [
        pltpu.VMEM((SIDE * 2 * rows, cols), BF),
        pltpu.VMEM((SIDE, rows, cols), BF),
        pltpu.VMEM((2, rows // 2, cols), BF),
        pltpu.VMEM((2, rows, cols), BF),
        pltpu.VMEM((3, rows, cols), BF),
        pltpu.VMEM((rows, cols), F32),
    ]


PAIR_ORDER = (2, 1, 3, 0)


class Pairs:
    def __init__(self, net, out, scr, far_first=True):
        self.net, self.out, self.scr, self.far_first = net, out, scr, far_first
        self.crossed = {}

    def store(self, dy, value):
        rows = value.shape[0]
        self.scr[0][pl.ds(dy * rows, rows), :] = value.astype(BF)

    def cross(self, dy):
        parts, other = self.scr[:2]
        c = here()[3]
        rows = other.shape[1]
        self.crossed[dy] = self.net.put(
            parts.at[span((2 * dy + 1 - c) * rows, rows)], other.at[dy], moved(dc=1)
        )

    def steps(self):
        net = self.net
        parts, other, through, landed, ready, total = self.scr
        c = here()[3]
        rows = total.shape[0]
        half = rows // 2
        first, last = pl.ds(0, half), pl.ds(half, half)

        def pair(dy, lo, size):
            mine = parts[span((2 * dy + c) * rows + lo, size), :].astype(F32)
            return mine + other[dy, pl.ds(lo, size), :].astype(F32)

        def far():
            self.crossed[2].wait_recv()
            ready[0] = pair(2, 0, rows).astype(BF)
            via_up = net.put(ready.at[0, first], through.at[0], moved(dy=1))
            via_down = net.put(ready.at[0, last], through.at[1], moved(dy=-1))
            return via_up, via_down

        if self.far_first:
            via_up, via_down = far()
            yield
        self.crossed[1].wait_recv()
        ready[1, last, :] = pair(1, half, half).astype(BF)
        up_late = net.put(ready.at[1, last], landed.at[0, last], moved(dy=1))
        yield
        self.crossed[3].wait_recv()
        ready[2, first, :] = pair(3, 0, half).astype(BF)
        down_first = net.put(ready.at[2, first], landed.at[1, first], moved(dy=-1))
        yield
        if not self.far_first:
            via_up, via_down = far()
            yield
        via_up.wait_recv()
        ready[1, first, :] = (pair(1, 0, half) + through[0].astype(F32)).astype(BF)
        up_first = net.put(ready.at[1, first], landed.at[0, first], moved(dy=1))
        via_down.wait_recv()
        ready[2, last, :] = (pair(3, half, half) + through[1].astype(F32)).astype(BF)
        down_late = net.put(ready.at[2, last], landed.at[1, last], moved(dy=-1))
        yield
        self.crossed[0].wait_recv()
        total[...] = pair(0, 0, rows)
        yield
        for copy in (up_late, down_first, up_first, down_late):
            copy.wait_recv()
        total[...] += landed[0].astype(F32) + landed[1].astype(F32)
        if self.out is not None:
            done = net.keep(total, self.out)
            yield
            done.wait()


def spread_narrow(net, low, slab, pieces):
    w = lax.axis_index("wide")
    n = lax.axis_index("narrow")
    base = n * ROWS if slab.shape[0] == TOK else w * TOK + n * ROWS
    mine, copies = [], []
    for start, stride, width, to in pieces:
        spot = slab.at[span(base, ROWS), pl.ds(to, width)]
        for p in NARROW_ALL:
            target = moved(**p)
            columns = lanes(start + target[1] * stride, width)
            copies.append(net.put(low.at[:, columns], spot, target))
        mine.append(net.keep(low.at[:, lanes(start + n * stride, width)], spot))
    yield
    for copy in mine:
        copy.wait()
    for copy in copies:
        copy.wait_recv()


SPREAD_COPIES = 7


def gather_wide(net, slab, lead, stage=None):
    x, z, y, c = here()
    rows = TOK // 2
    half = rows // 2
    low = 0 if lead == "x" else rows

    def block(a, b, lo=0, size=rows):
        px, pz = (a, b) if lead == "x" else (b, a)
        return slab.at[span((wrap(x + px) * SIDE + wrap(z + pz)) * TOK + low + lo, size)]

    def lead_to(d):
        return moved(dx=d) if lead == "x" else moved(dz=d)

    def then_to(d):
        return moved(dz=d) if lead == "x" else moved(dx=d)

    def both(src, to, dst=None):
        dst = src if dst is None else dst
        return net.put(src, dst, to(1)), net.put(src, dst, to(-1))

    mine = block(0, 0) if stage is None else stage.at[pl.ds(low, rows)]
    fore, aft = both(mine, lead_to, block(0, 0))
    second = {0: both(mine, then_to, block(0, 0))}
    yield
    fore.wait_recv()
    on = net.put(block(-1, 0, 0, half), block(-1, 0, 0, half), lead_to(1))
    second[-1] = both(block(-1, 0), then_to)
    aft.wait_recv()
    back = net.put(block(1, 0, half, half), block(1, 0, half, half), lead_to(-1))
    second[1] = both(block(1, 0), then_to)
    yield
    last = []

    def relay(a):
        f, b = second[a]
        f.wait_recv()
        last.append(net.put(block(a, -1, 0, half), block(a, -1, 0, half), then_to(1)))
        b.wait_recv()
        last.append(net.put(block(a, 1, half, half), block(a, 1, half, half), then_to(-1)))

    kept = None if stage is None else net.keep(mine, block(0, 0))
    relay(0)
    yield
    on.wait_recv()
    back.wait_recv()
    second[2] = both(block(2, 0), then_to)
    yield
    relay(-1)
    relay(1)
    yield
    relay(2)
    yield
    if kept is not None:
        kept.wait()
    for copy in last:
        copy.wait_recv()


WIDE_COPIES = 20


def mean_of(values):
    return jnp.sum(values, axis=-1, keepdims=True) * (1.0 / D)


def normal(values):
    centered = values - mean_of(values)
    inverse = lax.rsqrt(mean_of(centered * centered) + NORM_EPS)
    return centered * inverse, inverse


def normal_back(hat, inverse, d_hat):
    return inverse * (d_hat - mean_of(d_hat) - hat * mean_of(d_hat * hat))


def turn(values, cosine, sine):
    return values * cosine + pltpu.roll(values, HEAD_DIM // 2, 1) * sine


def allowed_keys(first_row, rows, first_length):
    query = first_row + lax.broadcasted_iota(jnp.int32, (rows, 1), 0)
    key = lax.broadcasted_iota(jnp.int32, (rows, GROUP), 1)
    start = jnp.where(query >= first_length, first_length, 0)
    return (key <= query) & (key >= start)


PICK_ATTN, PICK_FFN, GATE_FFN = 0, 32, 64
LATER_UNITS = 512


def branch_mask(marks, lane):
    n = lax.axis_index("narrow").astype(F32)
    return (n < 2.0 * (marks[:, lane : lane + 1] + 1.0)).astype(F32)


def half_turns(first_length, frequency, tv):
    rows = 64
    half = GROUP // 2
    left = lax.broadcasted_iota(jnp.int32, (rows, 128), 1) < HEAD_DIM // 2
    row = lax.broadcasted_iota(jnp.int32, (rows, 128), 0)

    @pl.loop(0, half // rows)
    def _(i):
        token = row + i * rows + jnp.where(left, 0, half)
        position = token - jnp.where(token >= first_length, first_length, 0)
        angles = position.astype(F32) * frequency
        cosine, sine = jnp.cos(angles), jnp.sin(angles)
        cosine_other = pltpu.roll(cosine, HEAD_DIM // 2, 1)
        sine_other = pltpu.roll(sine, HEAD_DIM // 2, 1)
        low, high = span(i * rows, rows), span(half + i * rows, rows)
        tv[0, low, :] = jnp.where(left, cosine, cosine_other)
        tv[0, high, :] = jnp.where(left, cosine_other, cosine)
        tv[1, low, :] = jnp.where(left, -sine, sine_other)
        tv[1, high, :] = jnp.where(left, -sine_other, sine)


GELU_SCALE = (2.0 / 3.141592653589793) ** 0.5
GELU_CUBE = 0.044715


def route(normed, first_layer, second_layer, picks):
    before = jnp.dot(normed, first_layer, preferred_element_type=F32)
    square = before * before
    bent = jnp.tanh(GELU_SCALE * before * (1.0 + GELU_CUBE * square))
    hidden = 0.5 * before * (1.0 + bent)
    slope = 0.5 * (1.0 + bent) + 0.5 * before * (1.0 - bent * bent) * GELU_SCALE * (
        1.0 + 3.0 * GELU_CUBE * square
    )
    logits = jnp.dot(hidden.astype(BF), second_layer, preferred_element_type=F32)
    lane = lax.broadcasted_iota(jnp.int32, logits.shape, 1)
    gates, logit_slopes, slopes = [], [], []
    for branch in range(2):
        start = branch * LEVELS
        inside = (lane >= start) & (lane < start + LEVELS)
        shown = jnp.where(inside, logits, -1e30)
        expo = jnp.exp(shown - jnp.max(shown, axis=-1, keepdims=True))
        expo = jnp.where(inside, expo, 0.0)
        probs = expo / jnp.sum(expo, axis=-1, keepdims=True)
        chosen = jnp.where(lane.astype(F32) == picks[branch] + float(start), 1.0, 0.0)
        gate = float(LEVELS) * jnp.sum(probs * chosen, axis=-1, keepdims=True)
        logit_slope = gate * (chosen - probs)
        gates.append(gate)
        logit_slopes.append(logit_slope)
        slopes.append(
            slope
            * lax.dot_general(
                logit_slope.astype(BF), second_layer, CONTRACT_COLS, preferred_element_type=F32
            )
        )
    return hidden, gates, logit_slopes, slopes


def attention_forward(
    tokens, picks, lengths, frequency, gains, router_in, router_out, master, upstream, cid
):
    pair_rows = 2 * TOK
    head_part = D // NARROW
    units = FF // NARROW
    low = jax.ShapeDtypeStruct((GROUP, head_part), BF)
    results = dict(
        attn_sum=jax.ShapeDtypeStruct((TOK, D), F32),
        q=low,
        k=low,
        v=low,
        p=jax.ShapeDtypeStruct((GROUP, 2 * GROUP), BF),
        a=low,
        g=jax.ShapeDtypeStruct((GROUP, D), BF),
        slab_a=jax.ShapeDtypeStruct((D, 4 * head_part), BF),
        slab_up=jax.ShapeDtypeStruct((D, units - LATER_UNITS), BF),
        stage_up=jax.ShapeDtypeStruct((TOK, LATER_UNITS), BF),
        slab_down=jax.ShapeDtypeStruct((D, units), BF),
        normed=jax.ShapeDtypeStruct((GROUP, D), BF),
        marks=jax.ShapeDtypeStruct((GROUP, 128), F32),
        after=jax.ShapeDtypeStruct((TOK, D), F32),
        second=jax.ShapeDtypeStruct((TOK, D), BF),
        d_act=jax.ShapeDtypeStruct((GROUP, units), F32),
        turns=jax.ShapeDtypeStruct((2, GROUP, HEAD_DIM), F32),
        router_low=jax.ShapeDtypeStruct((D, RH), BF),
        hidden=jax.ShapeDtypeStruct((TOK, RH), F32),
        gate=jax.ShapeDtypeStruct((TOK, 128), F32),
        logit_slopes=jax.ShapeDtypeStruct((2, TOK, 128), F32),
        slopes=jax.ShapeDtypeStruct((2, TOK, RH), F32),
    )
    held = tuple(k for k in results if k not in ("attn_sum", "slab_up", "stage_up"))
    own_inputs = (tokens, picks, lengths, frequency, gains, router_in, router_out)

    def body(net, ins, outs, scr):
        out = dict(zip(results, outs))
        to = dict(zip(held, scr))
        scr = scr[len(held) :]
        xv, wv, tv, mv = to["normed"], to["slab_a"], to["turns"], to["marks"]
        qv, kv, vv, pv, av = (to[k] for k in "qkvpa")
        held_in, scr = scr[:7], scr[7:]
        own_tokens, own_picks, lv, fv, own_gains, rv, ov = held_in
        stage_up, stage_down, normed_own, marks_own, full, low = scr[:6]
        pairs = scr[6:]
        master, upstream = ins[7:]
        x, z, y, c = here()
        master_load = net.keep(master, full)
        loads = [net.keep(a, b) for a, b in zip(ins[:7], held_in)]
        greet(NARROW_ALL + NEAR_XZ)
        sums = Pairs(net, out["attn_sum"], pairs)
        stores = []

        def store(*names):
            stores.extend([net.keep(to[name], out[name]) for name in names])

        moves = {
            SA: spread_narrow(
                net, low, wv, [(i * D, head_part, head_part, i * head_part) for i in range(4)]
            ),
            SU: spread_narrow(net, low, stage_up, [(4 * D, units, units - LATER_UNITS, 0)]),
            SL: spread_narrow(
                net,
                low,
                out["stage_up"],
                [(4 * D + units - LATER_UNITS, units, LATER_UNITS, 0)],
            ),
            SD: spread_narrow(net, low, stage_down, [(4 * D + FF, units, units, 0)]),
            GX: gather_narrow(net, normed_own, xv),
            GM: gather_narrow(net, marks_own, mv),
            GG: gather_narrow(net, upstream, to["g"]),
            WA: side_by_side(*[gather_wide(net, wv, k) for k in "xz"]),
            WU: side_by_side(*[gather_wide(net, out["slab_up"], k, stage_up) for k in "xz"]),
            WD: side_by_side(*[gather_wide(net, to["slab_down"], k, stage_down) for k in "xz"]),
            TOTAL: sums.steps(),
        }

        def cast():
            master_load.wait()

            @pl.loop(0, low.shape[1] // 2048)
            def _(i):
                columns = lanes(i * 2048, 2048)
                low[:, columns] = full[:, columns].astype(BF)

        def first_norm():
            for load in loads:
                load.wait()
            hat, _ = normal(own_tokens[...].astype(F32))
            normed_own[...] = (hat * own_gains[0:1, :]).astype(BF)

        def route_own():
            to["router_low"][...] = rv[...].astype(BF)
            row = lax.broadcasted_iota(jnp.int32, (TOK, TOK), 0)
            lane = lax.broadcasted_iota(jnp.int32, (TOK, TOK), 1)
            level = [
                jnp.sum(
                    jnp.where(row == lane, own_picks[b : b + 1, :].astype(F32), 0.0),
                    axis=-1,
                    keepdims=True,
                )
                for b in range(2)
            ]
            hidden, gates, logit_slopes, slopes = route(
                normed_own[...], to["router_low"][...], ov[...], level
            )
            to["hidden"][...] = hidden
            to["gate"][...] = jnp.broadcast_to(gates[0], (TOK, 128))
            for branch in range(2):
                to["logit_slopes"][branch] = logit_slopes[branch]
                to["slopes"][branch] = slopes[branch]
            other = jnp.where(lane < GATE_FFN, level[1], gates[1])
            marks_own[...] = jnp.where(lane < PICK_FFN, level[0], other)
            store("router_low", "hidden", "gate", "logit_slopes", "slopes")

        def tables():
            half_turns(lv[0:1, 0:1], fv[0:1, :], tv)
            store("turns")

        def down_back():
            store("g", "slab_down")

            @pl.loop(0, SIDE)
            def _(i):
                r = span(i * pair_rows, pair_rows)
                to["d_act"][r, :] = jnp.dot(
                    to["g"][r, :], to["slab_down"][...], preferred_element_type=F32
                )

            store("d_act")

        def project():
            store("normed", "slab_a")

            @pl.loop(0, SIDE)
            def _(i):
                r = span(i * pair_rows, pair_rows)
                proj = jnp.dot(xv[r, :], wv[:, : 3 * head_part], preferred_element_type=F32)
                cosine, sine = tv[0, r, :], tv[1, r, :]
                for h in range(2):
                    at = pl.ds(h * HEAD_DIM, HEAD_DIM)
                    a = h * HEAD_DIM
                    qv[r, at] = turn(proj[:, a : a + HEAD_DIM], cosine, sine).astype(BF)
                    a += head_part
                    kv[r, at] = turn(proj[:, a : a + HEAD_DIM], cosine, sine).astype(BF)
                vv[r, :] = proj[:, 2 * head_part :].astype(BF)

            store("q", "k", "v")

        def attend(dy):
            first = wrap(y + dy) * pair_rows
            r = span(first, pair_rows)
            allowed = allowed_keys(first, pair_rows, lv[0:1, 0:1])
            heads = []
            for h in range(2):
                at = pl.ds(h * HEAD_DIM, HEAD_DIM)
                scores = lax.dot_general(
                    qv[r, at], kv[:, at], CONTRACT_COLS, preferred_element_type=F32
                )
                scores = jnp.where(allowed, scores * HEAD_DIM ** (-0.5), -1e30)
                expo = jnp.exp(scores - jnp.max(scores, axis=-1, keepdims=True))
                probs = expo * (1.0 / jnp.sum(expo, axis=-1, keepdims=True))
                low = probs.astype(BF)
                pv[r, pl.ds(h * GROUP, GROUP)] = low
                heads.append(jnp.dot(low, vv[:, at], preferred_element_type=F32))
            mask = branch_mask(mv[r, :], PICK_ATTN)
            av[r, :] = (jnp.concatenate(heads, axis=1) * mask).astype(BF)
            back = lax.dot_general(
                av[r, :], wv[:, 3 * head_part :], CONTRACT_COLS, preferred_element_type=F32
            )
            sums.store(dy, back)
            sums.cross(dy)

        def second_norm():
            values = own_tokens[...].astype(F32) + to["gate"][:, :1] * sums.scr[5][...]
            to["after"][...] = values
            to["second"][...] = (normal(values)[0] * own_gains[1:2, :]).astype(BF)
            store("after", "second")

        works = {
            CA: cast,
            L1: first_norm,
            RF: route_own,
            TB: tables,
            Q: project,
            LN: second_norm,
            DA: down_back,
        }
        for dy in PAIR_ORDER:
            works[ATTEND[dy]] = functools.partial(attend, dy)
        follow(FORWARD_PLAN, works, moves)
        store("p", "a", "marks")
        for done in stores:
            done.wait()

    got = comm_call(
        body,
        list(own_inputs) + [master, upstream],
        list(results.values()),
        [pltpu.VMEM(results[k].shape, results[k].dtype) for k in held]
        + [pltpu.VMEM(r.shape, r.dtype) for r in own_inputs]
        + [
            pltpu.VMEM((TOK, units - LATER_UNITS), BF),
            pltpu.VMEM((TOK, units), BF),
            pltpu.VMEM((TOK, D), BF),
            pltpu.VMEM((TOK, 128), F32),
            pltpu.VMEM(master.shape, F32),
            pltpu.VMEM(master.shape, BF),
        ]
        + pairs_scratch(TOK, D),
        cid,
        REDUCE_COPIES + 6 * WIDE_COPIES + 3 * GATHER_COPIES + 7 * SPREAD_COPIES,
        8 + 7 + 3 + 4 + 1 + len(held),
        "attention_forward",
    )
    return dict(zip(results, got))


def first_scratch(cols):
    part, half = TOK // 2, TOK // 4
    return [
        pltpu.VMEM((2, 2, SIDE, half, cols), BF),
        pltpu.VMEM((2, 2, SIDE, part, cols), BF),
        pltpu.VMEM((2, 2, SIDE, half, cols), BF),
        pltpu.VMEM((2, SIDE, part, cols), BF),
    ]


def second_scratch(cols):
    part, half = TOK // 2, TOK // 4
    return [
        pltpu.VMEM((2, 2, half, cols), BF),
        pltpu.VMEM((2, 2, part, cols), BF),
        pltpu.VMEM((2, 2, half, cols), BF),
        pltpu.VMEM((TOK, cols), BF),
    ]


FIRST_COPIES = 12
SECOND_COPIES = 12
FIRST_LOCALS = 6


def lead_moves(lead):
    def lead_to(d):
        return moved(dx=d) if lead == "x" else moved(dz=d)

    def then_to(d):
        return moved(dz=d) if lead == "x" else moved(dx=d)

    return lead_to, then_to


def reduce_first(net, grad, scr, lead):
    via, landed, ready, sums = scr
    x, z, y, c = here()
    part, half = TOK // 2, TOK // 4
    k = 0 if lead == "x" else 1
    low = k * part
    blocks = grad.reshape(SIDE, SIDE, TOK, grad.shape[1])
    first, last = pl.ds(0, half), pl.ds(half, half)
    lead_to, _ = lead_moves(lead)

    def line(d, lo, size):
        rows = pl.ds(low + lo, size)
        if lead == "x":
            return (wrap(x + d), slice(None), rows, slice(None))
        return (slice(None), wrap(z + d), rows, slice(None))

    via_up = net.put(blocks.at[line(2, 0, half)], via.at[k, 0], lead_to(1))
    via_down = net.put(blocks.at[line(2, half, half)], via.at[k, 1], lead_to(-1))
    up_late = net.put(blocks.at[line(1, half, half)], landed.at[k, 0, :, last], lead_to(1))
    down_first = net.put(blocks.at[line(3, 0, half)], landed.at[k, 1, :, first], lead_to(-1))
    loads = [
        net.keep(blocks.at[line(1, 0, half)], ready.at[k, 0]),
        net.keep(blocks.at[line(3, half, half)], ready.at[k, 1]),
        net.keep(blocks.at[line(0, 0, part)], sums.at[k]),
    ]
    yield
    for load in loads:
        load.wait()
    via_up.wait_recv()

    @pl.loop(0, SIDE)
    def _(i):
        ready[k, 0, i] = (ready[k, 0, i].astype(F32) + via[k, 0, i].astype(F32)).astype(BF)

    up_first = net.put(ready.at[k, 0], landed.at[k, 0, :, first], lead_to(1))
    via_down.wait_recv()

    @pl.loop(0, SIDE)
    def _(i):
        ready[k, 1, i] = (ready[k, 1, i].astype(F32) + via[k, 1, i].astype(F32)).astype(BF)

    down_late = net.put(ready.at[k, 1], landed.at[k, 1, :, last], lead_to(-1))
    yield
    for copy in (up_late, down_first, up_first, down_late):
        copy.wait_recv()

    @pl.loop(0, SIDE)
    def _(i):
        both = landed[k, 0, i].astype(F32) + landed[k, 1, i].astype(F32)
        sums[k, i] = (sums[k, i].astype(F32) + both).astype(BF)


def reduce_second(net, sums, scr, lead):
    via, landed, ready, total = scr
    x, z, y, c = here()
    part, half = TOK // 2, TOK // 4
    k = 0 if lead == "x" else 1
    first, last = pl.ds(0, half), pl.ds(half, half)
    _, then_to = lead_moves(lead)
    me = z if lead == "x" else x

    def block(d, rows):
        return sums.at[k, wrap(me + d), rows]

    via_up = net.put(block(2, first), via.at[k, 0], then_to(1))
    via_down = net.put(block(2, last), via.at[k, 1], then_to(-1))
    up_late = net.put(block(1, last), landed.at[k, 0, last], then_to(1))
    down_first = net.put(block(3, first), landed.at[k, 1, first], then_to(-1))
    yield
    via_up.wait_recv()
    ready[k, 0] = (block(1, first)[...].astype(F32) + via[k, 0].astype(F32)).astype(BF)
    up_first = net.put(ready.at[k, 0], landed.at[k, 0, first], then_to(1))
    via_down.wait_recv()
    ready[k, 1] = (block(3, last)[...].astype(F32) + via[k, 1].astype(F32)).astype(BF)
    down_late = net.put(ready.at[k, 1], landed.at[k, 1, last], then_to(-1))
    yield
    for copy in (up_late, down_first, up_first, down_late):
        copy.wait_recv()
    both = landed[k, 0].astype(F32) + landed[k, 1].astype(F32)
    total[pl.ds(k * part, part), :] = (sums[k, me].astype(F32) + both).astype(BF)


def side_by_side(*parts):
    while True:
        if StopIteration in [next(part, StopIteration) for part in parts]:
            break
        yield


def return_narrow(net, total, out, pieces):
    n = lax.axis_index("narrow")
    copies, mine = [], []
    for start, width, to in pieces:
        spot = out.at[:, lanes(to + n * width, width)]
        columns = pl.ds(start, width)
        for p in NARROW_ALL:
            target = moved(**p)
            copies.append(net.put(total.at[span(target[1] * ROWS, ROWS), columns], spot, target))
        mine.append(net.keep(total.at[span(n * ROWS, ROWS), columns], spot))
    yield
    for copy in mine:
        copy.wait()
    for copy in copies:
        copy.wait_recv()


def second_then_narrow(net, sums, out, scr, pieces):
    yield from side_by_side(*[reduce_second(net, sums, scr, lead) for lead in "xz"])
    yield from return_narrow(net, scr[3], out, pieces)


def wide_then_narrow(net, grad, out, scr, pieces):
    yield from side_by_side(*[reduce_first(net, grad, scr[:4], lead) for lead in "xz"])
    yield from second_then_narrow(net, scr[3], out, scr[4:], pieces)


def feed_forward(normed_own, upstream, w_up, stage_up, w_down, d_act, marks, own, cid):
    pair_rows = 2 * TOK
    units = FF // NARROW
    strip = 256

    def body(net, ins, outs, scr):
        own, upstream, up_in, stage_in, down_in, da_in, marks = ins[:7]
        kept_up = up_in.shape[1]
        rest = pl.ds(kept_up, units - kept_up)
        ffn_part, g_up, down_sums, after_out, attn_out, hidden_out, vector_out = outs
        xv, dv, w_up, w_down, mv, act, du, da, gu, yv = scr[:10]
        gated, dots, dots_in = scr[16:19]
        held, d_attn, d_hidden, vector = scr[19:26], *scr[26:29]
        gds, firsts = scr[29:31], (scr[31:35], scr[35:39])
        stage = scr[39]
        n = lax.axis_index("narrow")
        x, z, y, c = here()
        loads = [
            net.keep(a, b)
            for a, b in (
                (stage_in, stage),
                (marks, mv),
                (up_in, w_up.at[:, pl.ds(0, kept_up)]),
                (da_in, da),
                (upstream, dv),
                (down_in, w_down),
            )
        ]
        own_loads = [net.keep(a, b) for a, b in zip(ins[7:], held)]
        greet(NARROW_ALL + NEAR_XZ)
        loads.pop(0).wait()
        sums = Pairs(net, None, scr[10:16], far_first=False)
        stores, dot_copies = [], []

        def gradient(left, right, to):
            @pl.loop(0, D // strip)
            def _(i):
                at = lanes(i * strip, strip)
                to[span(i * strip, strip), :] = lax.dot_general(
                    left[:, at], right[...], CONTRACT_ROWS, preferred_element_type=F32
                ).astype(BF)

        def wait_loads():
            for load in loads:
                load.wait()

        def half_gradient(i):
            columns = pl.ds(i * units // 2, units // 2)
            gradient(dv, gated.at[:, columns], gds[i])

        def units_of(dy, later):
            r = span(wrap(y + dy) * pair_rows, pair_rows)
            columns = rest if later else pl.ds(0, kept_up)
            up = jnp.dot(xv[r, :], w_up[:, columns], preferred_element_type=F32)
            positive = jnp.maximum(up, 0.0)
            masked = positive * branch_mask(mv[r, :], PICK_FFN)
            gate = mv[r, GATE_FFN : GATE_FFN + 1]
            active = positive * masked
            act[r, columns] = active.astype(BF)
            gated[r, columns] = (active * gate).astype(BF)
            back = da[r, columns]
            du[r, columns] = (back * (2.0 * gate * masked)).astype(BF)
            dot = lax.dot_general(
                jnp.ones((8, up.shape[1]), BF),
                (back * active).astype(BF),
                CONTRACT_COLS,
                preferred_element_type=F32,
            )
            for core in range(2):
                spot = wrap(y + dy) * 2 + core
                part = dot[:, core * TOK : (core + 1) * TOK]
                dots[spot] = dots[spot] + part if later else part

        def norm_back(dy):
            r = span(wrap(y + dy) * pair_rows, pair_rows)
            back = lax.dot_general(
                du[r, :], w_up[...], CONTRACT_COLS, preferred_element_type=F32
            )
            sums.store(dy, back)
            sums.cross(dy)

        def send_dots():
            for p in NARROW_ALL:
                target = moved(**p)
                dot_copies.append(net.put(dots.at[target[1]], dots_in.at[n], target))
            dots_in[n] = dots[n]

        def up_gradient():
            gradient(xv, du, gu)
            stores.append(net.keep(gu, g_up))

        def output(dy):
            r = span(wrap(y + dy) * pair_rows, pair_rows)
            yv[r, :] = lax.dot_general(
                act[r, :], w_down[...], CONTRACT_COLS, preferred_element_type=F32
            ).astype(BF)
            stores.append(net.keep(yv.at[r], ffn_part.at[r]))

        def second_norm_back():
            for load in own_loads:
                load.wait()
            for copy in dot_copies:
                copy.wait_recv()
            s = dots_in[0]
            for i in range(1, NARROW):
                s = s + dots_in[i]
            row = lax.broadcasted_iota(jnp.int32, (TOK, TOK), 0)
            lane = lax.broadcasted_iota(jnp.int32, (TOK, TOK), 1)
            ffn = jnp.sum(jnp.where(row == lane, s[0:1, :], 0.0), axis=-1, keepdims=True)
            after, attn, gate, gains, slopes, logit_slopes, hidden = held
            total = sums.scr[5]
            hat, inverse = normal(after[...])
            d_gain = jnp.sum(total[...] * hat, axis=0, keepdims=True)
            back = normal_back(hat, inverse, total[...] * gains[1:2, :])
            back = back + dv[span(n * TOK, TOK), :].astype(F32)
            total[...] = back
            d_attn[...] = (back * gate[:, :1]).astype(BF)
            attn_gate = jnp.sum(back * attn[...], axis=-1, keepdims=True)
            d_hidden[...] = (attn_gate * slopes[0] + ffn * slopes[1]).astype(BF)
            d_logits = attn_gate * logit_slopes[0] + ffn * logit_slopes[1]
            d_router = lax.dot_general(
                d_logits.astype(BF),
                hidden[...].astype(BF),
                CONTRACT_ROWS,
                preferred_element_type=F32,
            )
            vector[...] = jnp.zeros_like(vector)
            for i in range(GAIN_ROWS // 2):
                at = GAIN_ROWS // 2 + i
                vector[at : at + 1, :] = d_gain[:, i * 128 : (i + 1) * 128]
            for i in range(RH // 128):
                at = GAIN_ROWS + i * 2 * LEVELS
                vector[at : at + 2 * LEVELS, :] = d_router[: 2 * LEVELS, i * 128 : (i + 1) * 128]
            own_marks = mv[span(n * TOK, TOK), :]
            levels = lane.astype(F32)
            picked = jnp.where(levels == own_marks[:, PICK_ATTN : PICK_ATTN + 1], 1.0, 0.0)
            other = own_marks[:, PICK_FFN : PICK_FFN + 1] + float(LEVELS)
            picked = picked + jnp.where(levels == other, 1.0, 0.0)
            vector[SMALL_ROWS : SMALL_ROWS + 1, :] = jnp.sum(picked, axis=0, keepdims=True)
            pairs = zip(
                (total, d_attn, vector),
                (after_out, attn_out, vector_out),
            )
            stores.extend([net.keep(a, b) for a, b in pairs])

        works = {
            LD: wait_loads,
            GD: functools.partial(half_gradient, 0),
            GE: functools.partial(half_gradient, 1),
            GU: up_gradient,
            DS: send_dots,
            LB: second_norm_back,
        }
        for dy in PAIR_ORDER:
            works[EARLY[dy]] = functools.partial(units_of, dy, False)
            works[UNITS[dy]] = functools.partial(units_of, dy, True)
            works[OUTPUT[dy]] = functools.partial(output, dy)
            works[NORM[dy]] = functools.partial(norm_back, dy)
        moves = {
            GATHER: gather_narrow(net, own, xv),
            TOTAL: sums.steps(),
            FIRST: side_by_side(*[reduce_first(net, gds[0], firsts[0], lead) for lead in "xz"]),
            MORE: side_by_side(*[reduce_first(net, gds[1], firsts[1], lead) for lead in "xz"]),
            HID: gather_small(net, d_hidden, hidden_out),
            WU: side_by_side(*[gather_wide(net, w_up.at[:, rest], k, stage) for k in "xz"]),
        }
        follow(FEED_PLAN, works, moves)
        for i in range(2):
            columns = pl.ds(i * units // 2, units // 2)
            stores.append(net.keep(firsts[i][3], down_sums.at[:, :, :, columns]))
        for store in stores:
            store.wait()

    wide = pltpu.VMEM((GROUP, D), BF)
    tall = pltpu.VMEM((D, units), BF)
    square = pltpu.VMEM((GROUP, units), BF)
    return comm_call(
        body,
        [normed_own, upstream, w_up, stage_up, w_down, d_act, marks] + list(own),
        [
            jax.ShapeDtypeStruct((GROUP, D), BF),
            jax.ShapeDtypeStruct((D, units), BF),
            jax.ShapeDtypeStruct((2, SIDE, TOK // 2, units), BF),
            jax.ShapeDtypeStruct((TOK, D), F32),
            jax.ShapeDtypeStruct((TOK, D), BF),
            jax.ShapeDtypeStruct((GROUP, RH), BF),
            jax.ShapeDtypeStruct((VECTOR_ROWS, 128), F32),
        ],
        [wide, wide, tall, tall, pltpu.VMEM(marks.shape, F32), square, square]
        + [pltpu.VMEM((GROUP, units), F32), tall, wide]
        + pairs_scratch(TOK, D)
        + [square]
        + [pltpu.VMEM((NARROW, 8, TOK), F32)] * 2
        + [pltpu.VMEM(r.shape, r.dtype) for r in own]
        + [
            pltpu.VMEM((TOK, D), BF),
            pltpu.VMEM((TOK, RH), BF),
            pltpu.VMEM((VECTOR_ROWS, 128), F32),
        ]
        + [pltpu.VMEM((D, units // 2), BF)] * 2
        + first_scratch(units // 2) * 2
        + [pltpu.VMEM(stage_up.shape, BF)],
        cid,
        GATHER_COPIES + REDUCE_COPIES + 7 + 2 * FIRST_COPIES + 2 * WIDE_COPIES + GATHER_SMALL_COPIES,
        14 + 1 + 1 + 12 + 2 * FIRST_LOCALS + 2,
        "feed_forward",
    )


def squares_of(ref, rows, cols):
    s = jnp.zeros((SQUARE_ROWS, 128), F32)
    for i in range(ref.shape[0] // rows):
        for j in range(ref.shape[1] // cols):
            piece = ref[i * rows : (i + 1) * rows, j * cols : (j + 1) * cols].astype(F32)
            piece = piece * piece
            for a in range(rows // SQUARE_ROWS):
                for b in range(cols // 128):
                    s = s + piece[a * 8 : a * 8 + 8, b * 128 : b * 128 + 128]
    return s


def sum_everywhere(net, own, first, second, total):
    w = lax.axis_index("wide")
    n = lax.axis_index("narrow")

    def rows(i):
        return pl.ds(pl.multiple_of(i * 8, 8), 8)

    copies = []
    for p in NARROW_ALL:
        target = moved(**p)
        copies.append(net.put(own.at[rows(target[1])], first.at[n], target))
    first[n] = own[rows(n), :]
    for copy in copies:
        copy.wait_recv()
    s = first[0]
    for i in range(1, NARROW):
        s = s + first[i]
    second[w] = s
    copies = [net.put(second.at[w], second.at[w], moved(**p)) for p in WIDE_ALL]
    for copy in copies:
        copy.wait_recv()
    s = second[0]
    for i in range(1, WIDE):
        s = s + second[i]
    total[rows(n), :] = s
    copies = [net.put(total.at[rows(n)], total.at[rows(n)], moved(**p)) for p in NARROW_ALL]
    for copy in copies:
        copy.wait_recv()


def attention_backward(
    d_attn_own, ffn_part, g_up, down_sums, normed, hidden_in, own, kept, cid
):
    table_rows = D // NARROW
    pair_rows = 2 * TOK
    head_part = D // NARROW
    units = FF // NARROW
    strip = 256
    scale = HEAD_DIM ** (-0.5)
    scratch = (
        [pltpu.VMEM(r.shape, r.dtype) for r in kept]
        + [
            pltpu.VMEM((GROUP, D), BF),
            pltpu.VMEM((GROUP, head_part), F32),
            pltpu.VMEM((GROUP, head_part), F32),
            pltpu.VMEM((GROUP, 3 * head_part), BF),
            pltpu.VMEM((D, 3 * head_part), BF),
        ]
        + pairs_scratch(TOK, D)[1:]
        + reduce_scratch(TOK, D)
        + first_scratch(3 * head_part)
        + second_scratch(3 * head_part)
        + first_scratch(units)
        + second_scratch(units)
        + [pltpu.VMEM(down_sums.shape, BF)]
        + second_scratch(units)
        + [
            pltpu.VMEM((GROUP, table_rows), BF),
            pltpu.VMEM((GROUP, RH), BF),
            pltpu.VMEM((table_rows, RH), BF),
            pltpu.VMEM((WIDE, ROWS, RH), BF),
            pltpu.VMEM((ROWS, RH), BF),
            pltpu.VMEM((table_rows, RH), BF),
            pltpu.VMEM((1, D), F32),
        ]
        + [pltpu.VMEM(r.shape, r.dtype) for r in own]
        + [
            pltpu.VMEM((ROWS, 4 * D + 2 * FF), BF),
            pltpu.VMEM((TOK, D), BF),
            pltpu.VMEM((NARROW, 8, 128), F32),
            pltpu.VMEM((WIDE, 8, 128), F32),
            pltpu.VMEM((VECTOR_ROWS, 128), F32),
            pltpu.VMEM((8, 128), F32),
            pltpu.VMEM((D, head_part), BF),
        ]
        + first_scratch(head_part)
        + second_scratch(head_part)
    )

    def body(net, ins, outs, scr):
        d_attn_own, ffn_part, g_up, down_sums, normed, hidden_in = ins[:6]
        input_grad, result_out, block_out, table, vector_out, norm_out = outs
        wv, tv, mv, qv, kv, vv, pv, av = scr[:8]
        big, dk, dv, dproj, ga = scr[8:13]
        pairs, narrow = [big, *scr[13:18]], scr[18:24]
        wide_a, wide_up, wide_down = scr[24:32], scr[32:40], scr[40:45]
        columns, hidden, part, landed, shard, mine = scr[45:51]
        d_gain, held = scr[51], scr[52:58]
        block, result, first, second, summed, norm = scr[58:64]
        go, wide_o = scr[64], scr[65:73]
        n = lax.axis_index("narrow")
        x, z, y, c = here()
        first_load = net.keep(down_sums, wide_down[0])
        loads = [net.keep(a, b) for a, b in zip(ins[12:], scr[:8])]
        own_loads = [net.keep(a, b) for a, b in zip(ins[6:12], held)]
        loads.append(net.keep(hidden_in, hidden))
        loads.append(net.keep(normed.at[:, lanes(n * table_rows, table_rows)], columns))
        greet(NARROW_ALL + WIDE_ALL)
        sums = Pairs(net, None, pairs)
        thirds = [(i * head_part, head_part, i * D) for i in range(3)]

        def router():
            w = lax.axis_index("wide")
            part[...] = lax.dot_general(
                columns[...], hidden[...], CONTRACT_ROWS, preferred_element_type=F32
            ).astype(BF)
            copies = []
            for p in WIDE_ALL:
                target = moved(**p)
                rows = part.at[span(target[0] * ROWS, ROWS)]
                copies.append(net.put(rows, landed.at[w], target))
            kept = net.keep(part.at[span(w * ROWS, ROWS)], landed.at[w])
            yield
            kept.wait()
            for copy in copies:
                copy.wait_recv()
            s = landed[0].astype(F32)
            for i in range(1, WIDE):
                s = s + landed[i].astype(F32)
            shard[...] = s.astype(BF)
            spot = mine.at[span(w * ROWS, ROWS)]
            copies = [net.put(shard, spot, moved(**p)) for p in WIDE_ALL]
            kept = net.keep(shard, spot)
            yield
            kept.wait()
            for copy in copies:
                copy.wait_recv()
            yield from gather_narrow(net, mine, table)

        moves = {
            GATHER: gather_narrow(net, d_attn_own, big),
            DOWN: second_then_narrow(
                net, wide_down[0], block, wide_down[1:], [(0, units, 4 * D + FF)]
            ),
            UP: wide_then_narrow(net, g_up, block, wide_up, [(0, units, 4 * D)]),
            MIXED: wide_then_narrow(net, ga, block, wide_a, thirds),
            MO: wide_then_narrow(net, go, block, wide_o, [(0, head_part, 3 * D)]),
            FEED: reduce_narrow(net, ffn_part, narrow),
            GATES: router(),
            TOTAL: sums.steps(),
        }

        def wait_loads():
            first_load.wait()
            for load in loads:
                load.wait()
            dk[...] = jnp.zeros_like(dk)
            dv[...] = jnp.zeros_like(dv)

        def one_pair(dy):
            r = span(wrap(y + dy) * pair_rows, pair_rows)
            mask = branch_mask(mv[r, :], PICK_ATTN)
            back = jnp.dot(big[r, :], wv[:, 3 * head_part :], preferred_element_type=F32)
            back = (back * mask).astype(BF)
            for h in range(2):
                at = pl.ds(h * HEAD_DIM, HEAD_DIM)
                d_out = back[:, h * HEAD_DIM : (h + 1) * HEAD_DIM]
                d_probs = lax.dot_general(
                    d_out, vv[:, at], CONTRACT_COLS, preferred_element_type=F32
                )
                probs_low = pv[r, pl.ds(h * GROUP, GROUP)]
                probs = probs_low.astype(F32)
                weighted = probs * d_probs
                centre = jnp.sum(weighted, axis=-1, keepdims=True)
                ds = (weighted - probs * centre).astype(BF)
                dq = jnp.dot(ds, kv[:, at], preferred_element_type=F32) * scale
                dproj[r, at] = turn(dq, tv[0, r, :], -tv[1, r, :]).astype(BF)
                dk[:, at] += lax.dot_general(
                    ds, qv[r, at], CONTRACT_ROWS, preferred_element_type=F32
                )
                dv[:, at] += lax.dot_general(
                    probs_low, d_out, CONTRACT_ROWS, preferred_element_type=F32
                )

        refill = []

        def turn_back():
            refill.append(net.keep(normed, pv))

            @pl.loop(0, SIDE)
            def _(i):
                r = span(i * pair_rows, pair_rows)
                cosine, sine = tv[0, r, :], -tv[1, r, :]
                for h in range(2):
                    at = pl.ds(h * HEAD_DIM, HEAD_DIM)
                    to = pl.ds(head_part + h * HEAD_DIM, HEAD_DIM)
                    dproj[r, to] = turn(dk[r, at] * scale, cosine, sine).astype(BF)
                dproj[r, pl.ds(2 * head_part, head_part)] = dv[r, :].astype(BF)

        def gradient(left, right, to):
            @pl.loop(0, D // strip)
            def _(i):
                to[span(i * strip, strip), :] = lax.dot_general(
                    left[:, lanes(i * strip, strip)],
                    right[...],
                    CONTRACT_ROWS,
                    preferred_element_type=F32,
                ).astype(BF)

        def mixed_gradient():
            refill[0].wait()
            gradient(pv, dproj, ga)

        def norm_back(dy):
            r = span(wrap(y + dy) * pair_rows, pair_rows)
            back = lax.dot_general(
                dproj[r, :], wv[:, : 3 * head_part], CONTRACT_COLS, preferred_element_type=F32
            )
            sums.store(dy, back)
            sums.cross(dy)

        stores = []

        own_there = []

        def wait_own():
            if not own_there:
                own_there.append(True)
                for load in own_loads:
                    load.wait()

        def output():
            wait_own()
            gate = mv[span(n * TOK, TOK), GATE_FFN : GATE_FFN + 1]
            result[...] = (held[4][...] + gate * narrow[5][...]).astype(BF)
            stores.append(net.keep(result, result_out))

        squares = []

        def late_squares():
            squares.append(squares_of(block.at[:, pl.ds(3 * D, D + 2 * FF)], ROWS, 2048))

        def first_norm_back():
            wait_own()
            tokens, after, gains, router_in = held[:4]
            total = sums.scr[5]
            d_normed = total[...] + lax.dot_general(
                hidden[span(n * TOK, TOK), :],
                router_in[...],
                CONTRACT_COLS,
                preferred_element_type=F32,
            )
            hat, inverse = normal(tokens[...].astype(F32))
            d_gain[...] = jnp.sum(d_normed * hat, axis=0, keepdims=True)
            total[...] = after[...] + normal_back(hat, inverse, d_normed * gains[0:1, :])
            stores.append(net.keep(total, input_grad))

        works = {
            LB: first_norm_back,
            OUT: output,
            SQ: late_squares,
            LD: wait_loads,
            RT: turn_back,
            GO: functools.partial(gradient, big, av, go),
            GQ: mixed_gradient,
        }
        for dy in PAIR_ORDER:
            works[PAIR[dy]] = functools.partial(one_pair, dy)
            works[NORM[dy]] = functools.partial(norm_back, dy)
        follow(BACKWARD_PLAN, works, moves)
        stores.append(net.keep(block, block_out))
        vector = held[5]
        for i in range(GAIN_ROWS // 2):
            vector[i : i + 1, :] = d_gain[:, i * 128 : (i + 1) * 128]
        others = squares_of(block.at[:, pl.ds(0, 3 * D)], ROWS, 2048)
        others = others + squares_of(shard, ROWS, RH)
        vector[VECTOR_ROWS - SQUARE_ROWS :, :] = squares[0] + others
        sum_everywhere(net, vector, first, second, summed)
        stores.append(net.keep(summed, vector_out))
        s = summed[...]
        small = s[:SMALL_ROWS]
        sum_all = jnp.sum(small * small) + jnp.sum(s[VECTOR_ROWS - SQUARE_ROWS :])
        norm[...] = jnp.sqrt(jnp.full((8, 128), sum_all, F32))
        stores.append(net.keep(norm, norm_out))
        for store in stores:
            store.wait()

    return comm_call(
        body,
        [d_attn_own, ffn_part, g_up, down_sums, normed, hidden_in] + list(own) + list(kept),
        [
            jax.ShapeDtypeStruct((TOK, D), F32),
            jax.ShapeDtypeStruct((TOK, D), BF),
            jax.ShapeDtypeStruct((ROWS, 4 * D + 2 * FF), BF),
            jax.ShapeDtypeStruct((D, RH), BF),
            jax.ShapeDtypeStruct((VECTOR_ROWS, 128), F32),
            jax.ShapeDtypeStruct((8, 128), F32),
        ],
        scratch,
        cid,
        GATHER_COPIES
        + 2 * REDUCE_COPIES
        + 3 * FIRST_COPIES
        + 4 * SECOND_COPIES
        + 6 * 7
        + 2 * 15
        + GATHER_COPIES
        + 7 + 15 + 7,
        17 + 1 + 1 + 5 + REDUCE_LOCALS + 3 * FIRST_LOCALS + 6 + 4,
        "attention_backward",
    )


def adamw(weight, moment_one, moment_two, gradient, step_rate):
    one = 0.9 * moment_one + 0.1 * gradient
    two = 0.95 * moment_two + 0.05 * (gradient * gradient)
    scaled = jnp.maximum(two * (1.0 / (1.0 - 0.95**STEP)), 1e-30)
    root = scaled * lax.rsqrt(scaled) + 1e-08
    guess = pltpu.reciprocal(root, approx=True)
    guess = guess * (2.0 - root * guess)
    guess = guess * (2.0 - root * guess)
    rate = step_rate / (1.0 - 0.9**STEP)
    updated = weight * (1.0 - step_rate * 0.1) - (one * rate) * guess
    return updated, one, two


def clip_of(norm):
    return jnp.minimum(1.0, CLIP_NORM / norm[0:1, 0:1])


def all_steps(block, layer, gains, second_layer, vector, norm):
    block_parts, layer_parts = 3, 2
    n_loads = 4 * (block_parts + layer_parts)

    def kernel(*refs):
        block_in, layer_in = refs[0:4], refs[4:8]
        gains_in, second_in, vec, n = refs[8:11], refs[11:14], refs[14], refs[15]
        block_out, layer_out = refs[16:20], refs[20:23]
        gains_out, second_out, counts_out, norm_out = refs[23:26], refs[26:29], refs[29], refs[30]
        held_block, held_layer, new_block, new_layer = (
            refs[31:35],
            refs[35:39],
            refs[39:43],
            refs[43:46],
        )
        gain_grad, second_grad, loaded, stored = refs[46:50]
        clip = clip_of(n)

        def start(pairs, part, sems, at):
            copies = []
            for i, (a, b) in enumerate(pairs):
                copies.append(pltpu.make_async_copy(a.at[part], b.at[part], sems.at[at + i]))
                copies[-1].start()
            return copies

        parts = []
        for i in range(block_parts):
            cols = block_in[0].shape[1] // block_parts
            parts.append((True, (slice(None), pl.ds(i * cols, cols))))
        for i in range(layer_parts):
            rows = layer_in[0].shape[0] // layer_parts
            parts.append((False, (pl.ds(i * rows, rows), slice(None))))
        loads, stores = [], []
        for i, (is_block, part) in enumerate(parts):
            pairs = zip(block_in, held_block) if is_block else zip(layer_in, held_layer)
            loads.append(start(pairs, part, loaded, 4 * i))

        for i in range(GAIN_ROWS):
            row, at = i // (GAIN_ROWS // 2), i % (GAIN_ROWS // 2) * 128
            gain_grad[row : row + 1, at : at + 128] = vec[i : i + 1, :]
        for i in range(RH // 128):
            at = GAIN_ROWS + i * 2 * LEVELS
            second_grad[:, i * 128 : (i + 1) * 128] = vec[at : at + 2 * LEVELS, :]
        for held, grad, new, rate in (
            (gains_in, gain_grad, gains_out, 0.6),
            (second_in, second_grad, second_out, 0.02),
        ):
            results = adamw(*[r[...] for r in held], grad[...] * clip, rate)
            for ref, value in zip(new, results):
                ref[...] = value
        row = vec[SMALL_ROWS : SMALL_ROWS + 1, :]
        counts_out[0:1, :] = row[:, :LEVELS]
        counts_out[1:2, :] = pltpu.roll(row, 128 - LEVELS, 1)[:, :LEVELS]
        norm_out[...] = n[0:1, 0:1]

        for i, (is_block, part) in enumerate(parts):
            for copy in loads[i]:
                copy.wait()
            held, new = (held_block, new_block) if is_block else (held_layer, new_layer)
            gradient = held[3][part].astype(F32) * clip
            results = adamw(*[r[part] for r in held[:3]], gradient, 0.02)
            for ref, value in zip(new, results):
                ref[part] = value
            if is_block:
                new[3][part] = results[0].astype(BF)
            pairs = zip(new, block_out if is_block else layer_out)
            stores += start(pairs, part, stored, 4 * i)
        for copy in stores:
            copy.wait()

    def like(x, dtype=F32):
        return jax.ShapeDtypeStruct(x.shape, dtype)

    def room(x, dtype=F32):
        return pltpu.VMEM(x.shape, dtype)

    far, near = pl.BlockSpec(memory_space=pl.ANY), pl.BlockSpec(memory_space=pltpu.VMEM)
    b, r, g, o = block[0], layer[0], gains[0], second_layer[0]
    return pl.pallas_call(
        kernel,
        out_shape=[like(b)] * 3
        + [like(b, BF)]
        + [like(r)] * 3
        + [like(g)] * 3
        + [like(o)] * 3
        + [jax.ShapeDtypeStruct((2, LEVELS), F32), jax.ShapeDtypeStruct((1, 1), F32)],
        in_specs=[far] * 8 + [near] * 8,
        out_specs=[far] * 7 + [near] * 8,
        scratch_shapes=[room(b)] * 3
        + [room(b, BF)]
        + [room(r)] * 3
        + [room(r, BF)]
        + [room(b)] * 3
        + [room(b, BF)]
        + [room(r)] * 3
        + [room(g), room(o)]
        + [pltpu.SemaphoreType.DMA((n_loads,)), pltpu.SemaphoreType.DMA((n_loads,))],
        compiler_params=pltpu.CompilerParams(vmem_limit_bytes=60 * 2**20),
        name="all_steps",
    )(*block, *layer, *gains, *second_layer, vector, norm)


def on_device(
    tokens,
    lengths,
    picks,
    cotangent,
    block_master,
    block_first,
    block_second,
    gains,
    gains_first,
    gains_second,
    router_in,
    router_in_first,
    router_in_second,
    router_out,
    router_out_first,
    router_out_second,
):
    half_dim = HEAD_DIM // 2
    angle_steps = 10000.0 ** (-np.arange(half_dim, dtype=np.float32) / half_dim)
    frequency = jnp.asarray(np.tile(angle_steps.astype(np.float32), (8, 2)))
    f = attention_forward(
        tokens,
        picks.T,
        lengths,
        frequency,
        gains,
        router_in,
        jnp.pad(router_out, ((0, 0), (0, 128 - 2 * LEVELS))).astype(BF),
        block_master,
        cotangent,
        1,
    )

    ffn_part, grad_up, down_sums, d_after, d_attn, d_hidden, vector = feed_forward(
        f["second"],
        f["g"],
        f["slab_up"],
        f["stage_up"],
        f["slab_down"],
        f["d_act"],
        f["marks"],
        [f["after"], f["attn_sum"], f["gate"], gains, f["slopes"], f["logit_slopes"], f["hidden"]],
        2,
    )
    d_inputs, result, block_low, router_in_grad, vector, norm = attention_backward(
        d_attn,
        ffn_part,
        grad_up,
        down_sums,
        f["normed"],
        d_hidden,
        [tokens, d_after, gains, f["router_low"], f["after"], vector],
        [f[k] for k in ("slab_a", "turns", "marks", "q", "k", "v", "p", "a")],
        3,
    )
    (
        new_block,
        new_block_first,
        new_block_second,
        block_copy,
        new_router_in,
        new_router_in_first,
        new_router_in_second,
        new_gains,
        new_gains_first,
        new_gains_second,
        new_router_out,
        new_router_out_first,
        new_router_out_second,
        counts,
        grad_norm,
    ) = all_steps(
        (block_master, block_first, block_second, block_low),
        (router_in, router_in_first, router_in_second, router_in_grad),
        (gains, gains_first, gains_second),
        (router_out.T, router_out_first.T, router_out_second.T),
        vector,
        norm,
    )
    return (
        result,
        d_inputs,
        counts,
        grad_norm.reshape(()),
        new_block,
        new_block_first,
        new_block_second,
        block_copy,
        new_gains,
        new_gains_first,
        new_gains_second,
        new_router_in,
        new_router_in_first,
        new_router_in_second,
        new_router_out.T,
        new_router_out_first.T,
        new_router_out_second.T,
    )


def solution(mesh):
    both = P(("wide", "narrow"), None)
    return jax.shard_map(
        on_device,
        mesh=mesh,
        in_specs=(both, P("wide", None)) + (both,) * 5 + (P(),) * 9,
        out_specs=(both, both, P(), P()) + (both,) * 4 + (P(),) * 9,
        check_vma=False,
    )
```

profile of v0, /device:TPU:1, one launch (start us, length us, event | category | flops | bytes accessed | tf_op | source)
XLA Modules:
  0.0 256.2 jit_solution(14034959718941026743)
XLA Ops:
  0.7 0.7 convert.4
  1.4 0.1 copy.35
  1.5 0.6 pad.5.refs_6_
  2.1 90.2 %attention_forward.1 = (f32[128,2048]{1,0:T(8,128)}, bf16[1024,256]{1,0:T(8,128)(2,1)}, bf16[1024,256]{1,0:T(8,128)(2,1)}, bf16[1024,256]{1,0:T(8,128)(2,1)}, bf...) custom-call(bf16[128,2048]{1,0:T(8,128)(2,1)} %refs_6_.2, ...), custom_call_target="tpu_custom_call" | custom-call | tf_op jit(solution)/shard_map/attention_forward/pallas_call | solution.py:193
  92.3 63.2 %feed_forward.1 = (bf16[1024,2048]{1,0:T(8,128)(2,1)}, bf16[2048,1024]{1,0:T(8,128)(2,1)}, bf16[2,4,64,1024]{3,2,1,0:T(8,128)(2,1)}, f32[128,2048]{1,0:T(8,128)}...) custom-call(bf16[128,2048]{1,0:T(8,128)(2,1)} %get-tuple-element.67.refs_0_, ...), custom_call_target="tpu_custom_call" | custom-call | tf_op jit(solution)/shard_map/feed_forward/pallas_call | solution.py:193
  155.5 87.5 %attention_backward.1 = (f32[128,2048]{1,0:T(8,128)}, bf16[128,2048]{1,0:T(8,128)(2,1)}, bf16[16,24576]{1,0:T(8,128)(2,1)}, bf16[2048,256]{1,0:T(8,128)(2,1)}, f32[64,128]{1,0:T(8,128)}, /*index=5*/f32[8,128]{1,0:T(8,128)}) custom-call(bf16[128,2048]{1,0:T(8,128)(2,1)} %get-tuple-element.80.refs_0_, bf16[1024,2048]{1,0:T(8,128)(2,1)} %get-tuple-element.81.refs_1_, ...), custom_call_target="tpu_custom_call" | custom-call | tf_op jit(solution)/shard_map/attention_backward/pallas_call | solution.py:193
  243.1 0.0 copy-start.1
  243.1 0.0 copy-start
  243.1 11.1 %all_steps.1 = (f32[16,24576]{1,0:T(8,128)}, f32[16,24576]{1,0:T(8,128)}, f32[16,24576]{1,0:T(8,128)}, bf16[16,24576]{1,0:T(8,128)(2,1)}, f32[2048,256]{1,0:T(8,...) custom-call(f32[16,24576]{1,0:T(8,128)} %refs_0_.3, ...), custom_call_target="tpu_custom_call" | custom-call | tf_op jit(solution)/shard_map/all_steps/pallas_call | solution.py:1611
  254.2 0.0 copy-done.1
  254.2 0.8 copy.38
  255.0 0.0 copy-done
  255.0 1.0 copy.39
Async XLA Ops:
  243.1 11.1 %copy-start.1 = (bf16[128,2048]{1,0:T(8,128)(2,1)S(1)}, bf16[128,2048]{1,0:T(8,128)(2,1)}, u32[]{:S(2)}) copy-start(bf16[128,2048]{1,0:T(8,128)(2,1)} %get-tuple-element.134) | copy-start | bytes 1572868
  243.1 11.9 %copy-start = (f32[128,2048]{1,0:T(8,128)S(1)}, f32[128,2048]{1,0:T(8,128)}, u32[]{:S(2)}) copy-start(f32[128,2048]{1,0:T(8,128)} %get-tuple-element.135) | copy-start | bytes 3145732
where the time goes:
time: 260 us; the launch traced here: 256 us
  Pallas kernels  252 us (97%)
    pallas_call x3, Pallas kernels, comm_call(): pl.pallas_call(kernel, out_shape=outs, in_specs=[pl.BlockSpec(memory_spac...  241 us
    pallas_call x1, Pallas kernels, all_steps(): pl.pallas_call(kernel, out_shape=[like(b)] * 3 + [like(b, BF)] + [like(r)...  11.1 us

commit v1 on v0

--- a/solution.py
+++ b/solution.py
@@ -37,10 +37,11 @@
 
 
 (
-    CA, DA, DOWN, DS, FEED, FIRST, GATES, GATHER, GD, GE, GG, GM, GO, GQ, GU, GX, HID, L1, LB,
-    LD, LN, MIXED, MO, MORE, N0, N1, N2, N3, OUT, P0, P1, P2, P3, Q, RF, RT, SA, SD, SL, SQ, SU,
-    T0, T1, T2, T3, TB, TOTAL, U0, U1, U2, U3, UP, V0, V1, V2, V3, WA, WD, WU, Y0, Y1, Y2, Y3,
-) = range(63)
+    CA, DA, DOWN, DS, EX, FEED, FIRST, GATES, GATHER, GD, GE, GG, GM, GO, GQ, GU, GX, HID, L1,
+    LB, LD, LN, MIXED, MO, MORE, N0, N1, N2, N3, OUT, P0, P1, P2, P3, Q, RF, RT, SA, SD, SL, SQ,
+    SU, T0, T1, T2, T3, TB, TOTAL, U0, U1, U2, U3, UP, V0, V1, V2, V3, WA, WD, WU, Y0, Y1, Y2,
+    Y3,
+) = range(64)
 ATTEND = (T0, T1, T2, T3)
 EARLY = (V0, V1, V2, V3)
 UNITS = (U0, U1, U2, U3)
@@ -50,10 +51,10 @@
 
 
 FORWARD_PLAN = (
-    CA, SA, L1, SU, RF, GM, SD, GM, SA, WA, GM, GX, WA, SU, GX, WA, GM, GM, WA, GX, WA, SD, GG,
-    SL, WA, WU, GX, WD, GX, GM, GX, WU, WA, TB, GG, Q, WD, GM, GG, T2, T1, WD, TOTAL, T3, T0,
-    TOTAL, WD, TOTAL, WD, GX, GG, SL, GG, WD, WU, TOTAL, WU, WU, WD, GG, DA, WU, GG, TOTAL,
-    TOTAL, LN, WU, TOTAL, WU, GG,
+    CA, SA, L1, TB, GX, SA, GX, WA, RF, GM, WA, WA, GX, GX, SU, WA, SD, WA, GX, GG, GM, WA, SD,
+    GG, WD, SU, GX, SL, GM, WU, EX, WA, Q, WD, T1, GG, WU, T2, WD, TOTAL, T0, WD, T3, TOTAL, WD,
+    TOTAL, GG, TOTAL, WD, WU, TOTAL, GG, GG, WU, WD, DA, WU, GG, TOTAL, WU, LN, WU, GX, SL,
+    TOTAL, GG, WU,
 )
 FEED_PLAN = (
     GATHER, WU, WU, GATHER, WU, LD, GATHER, WU, WU, V0, WU, GATHER, V1, WU, V3, U1, GATHER, U3,
@@ -663,8 +664,8 @@
         qv, kv, vv, pv, av = (to[k] for k in "qkvpa")
         held_in, scr = scr[:7], scr[7:]
         own_tokens, own_picks, lv, fv, own_gains, rv, ov = held_in
-        stage_up, stage_down, normed_own, marks_own, full, low = scr[:6]
-        pairs = scr[6:]
+        stage_up, stage_down, normed_own, marks_own, full, low, mark_rows = scr[:7]
+        pairs = scr[7:]
         master, upstream = ins[7:]
         x, z, y, c = here()
         master_load = net.keep(master, full)
@@ -689,7 +690,7 @@
             ),
             SD: spread_narrow(net, low, stage_down, [(4 * D + FF, units, units, 0)]),
             GX: gather_narrow(net, normed_own, xv),
-            GM: gather_narrow(net, marks_own, mv),
+            GM: gather_small(net, marks_own, mark_rows),
             GG: gather_narrow(net, upstream, to["g"]),
             WA: side_by_side(*[gather_wide(net, wv, k) for k in "xz"]),
             WU: side_by_side(*[gather_wide(net, out["slab_up"], k, stage_up) for k in "xz"]),
@@ -731,9 +732,29 @@
             for branch in range(2):
                 to["logit_slopes"][branch] = logit_slopes[branch]
                 to["slopes"][branch] = slopes[branch]
-            other = jnp.where(lane < GATE_FFN, level[1], gates[1])
-            marks_own[...] = jnp.where(lane < PICK_FFN, level[0], other)
+            marks_own[...] = jnp.zeros_like(marks_own)
+            for b in range(2):
+                marks_own[b : b + 1, :] = own_picks[b : b + 1, :].astype(F32)
+            marks_own[2:3, :] = jnp.sum(
+                jnp.where(row == lane, gates[1], 0.0), axis=0, keepdims=True
+            )
             store("router_low", "hidden", "gate", "logit_slopes", "slopes")
+
+        def expand():
+            row = lax.broadcasted_iota(jnp.int32, (TOK, TOK), 0)
+            lane = lax.broadcasted_iota(jnp.int32, (TOK, TOK), 1)
+
+            @pl.loop(0, NARROW)
+            def _(i):
+                rows = mark_rows[span(i * ROWS, ROWS), :]
+                marks = [
+                    jnp.sum(jnp.where(row == lane, rows[b : b + 1, :], 0.0), axis=1, keepdims=True)
+                    for b in range(3)
+                ]
+                other = jnp.where(lane < GATE_FFN, marks[1], marks[2])
+                mv[span(i * TOK, TOK), :] = jnp.where(lane < PICK_FFN, marks[0], other)
+
+            store("marks")
 
         def tables():
             half_turns(lv[0:1, 0:1], fv[0:1, :], tv)
@@ -792,6 +813,8 @@
             )
             sums.store(dy, back)
             sums.cross(dy)
+            stores.append(net.keep(pv.at[r], out["p"].at[r]))
+            stores.append(net.keep(av.at[r], out["a"].at[r]))
 
         def second_norm():
             values = own_tokens[...].astype(F32) + to["gate"][:, :1] * sums.scr[5][...]
@@ -803,6 +826,7 @@
             CA: cast,
             L1: first_norm,
             RF: route_own,
+            EX: expand,
             TB: tables,
             Q: project,
             LN: second_norm,
@@ -811,7 +835,6 @@
         for dy in PAIR_ORDER:
             works[ATTEND[dy]] = functools.partial(attend, dy)
         follow(FORWARD_PLAN, works, moves)
-        store("p", "a", "marks")
         for done in stores:
             done.wait()
 
@@ -825,14 +848,15 @@
             pltpu.VMEM((TOK, units - LATER_UNITS), BF),
             pltpu.VMEM((TOK, units), BF),
             pltpu.VMEM((TOK, D), BF),
-            pltpu.VMEM((TOK, 128), F32),
+            pltpu.VMEM((ROWS, 128), F32),
             pltpu.VMEM(master.shape, F32),
             pltpu.VMEM(master.shape, BF),
+            pltpu.VMEM((NARROW * ROWS, 128), F32),
         ]
         + pairs_scratch(TOK, D),
         cid,
         REDUCE_COPIES + 6 * WIDE_COPIES + 3 * GATHER_COPIES + 7 * SPREAD_COPIES,
-        8 + 7 + 3 + 4 + 1 + len(held),
+        8 + 7 + 3 + 4 + 1 + 8 + len(held),
         "attention_forward",
     )
     return dict(zip(results, got))

time: 260 us -> 257 us (0.988)
  Pallas kernels: 252 us -> 249 us
    pallas_call x3, Pallas kernels: 241 us -> 238 us  [comm_call(): pl.pallas_call(kernel, out_shape=outs, in_specs=[pl.BlockSpec(memory_spac...]
where the time goes in v1:
time: 257 us; the launch traced here: 253 us
  Pallas kernels  249 us (97%)
    pallas_call x3, Pallas kernels, comm_call(): pl.pallas_call(kernel, out_shape=outs, in_specs=[pl.BlockSpec(memory_spac...  238 us
    pallas_call x1, Pallas kernels, all_steps(): pl.pallas_call(kernel, out_shape=[like(b)] * 3 + [like(b, BF)] + [like(r)...  11.1 us

profile of v1, /device:TPU:1, one launch (start us, length us, event | category | flops | bytes accessed | tf_op | source)
XLA Modules:
  0.0 253.0 jit_solution(7509402541566710841)
XLA Ops:
  0.7 0.7 convert.4
  1.4 0.1 copy.35
  1.5 0.6 pad.5.refs_6_
  2.1 88.0 %attention_forward.1 = (f32[128,2048]{1,0:T(8,128)}, bf16[1024,256]{1,0:T(8,128)(2,1)}, bf16[1024,256]{1,0:T(8,128)(2,1)}, bf16[1024,256]{1,0:T(8,128)(2,1)}, bf...) custom-call(bf16[128,2048]{1,0:T(8,128)(2,1)} %refs_6_.2, ...), custom_call_target="tpu_custom_call" | custom-call | tf_op jit(solution)/shard_map/attention_forward/pallas_call | solution.py:194
  90.1 61.9 %feed_forward.1 = (bf16[1024,2048]{1,0:T(8,128)(2,1)}, bf16[2048,1024]{1,0:T(8,128)(2,1)}, bf16[2,4,64,1024]{3,2,1,0:T(8,128)(2,1)}, f32[128,2048]{1,0:T(8,128)}...) custom-call(bf16[128,2048]{1,0:T(8,128)(2,1)} %get-tuple-element.67.refs_0_, ...), custom_call_target="tpu_custom_call" | custom-call | tf_op jit(solution)/shard_map/feed_forward/pallas_call | solution.py:194
  152.1 87.8 %attention_backward.1 = (f32[128,2048]{1,0:T(8,128)}, bf16[128,2048]{1,0:T(8,128)(2,1)}, bf16[16,24576]{1,0:T(8,128)(2,1)}, bf16[2048,256]{1,0:T(8,128)(2,1)}, f32[64,128]{1,0:T(8,128)}, /*index=5*/f32[8,128]{1,0:T(8,128)}) custom-call(bf16[128,2048]{1,0:T(8,128)(2,1)} %get-tuple-element.80.refs_0_, bf16[1024,2048]{1,0:T(8,128)(2,1)} %get-tuple-element.81.refs_1_, ...), custom_call_target="tpu_custom_call" | custom-call | tf_op jit(solution)/shard_map/attention_backward/pallas_call | solution.py:194
  239.9 0.0 copy-start.1
  239.9 0.0 copy-start
  239.9 11.1 %all_steps.1 = (f32[16,24576]{1,0:T(8,128)}, f32[16,24576]{1,0:T(8,128)}, f32[16,24576]{1,0:T(8,128)}, bf16[16,24576]{1,0:T(8,128)(2,1)}, f32[2048,256]{1,0:T(8,...) custom-call(f32[16,24576]{1,0:T(8,128)} %refs_0_.3, ...), custom_call_target="tpu_custom_call" | custom-call | tf_op jit(solution)/shard_map/all_steps/pallas_call | solution.py:1635
  251.0 0.0 copy-done.1
  251.0 0.8 copy.38
  251.8 0.0 copy-done
  251.8 1.0 copy.39
Async XLA Ops:
  239.9 11.1 %copy-start.1 = (bf16[128,2048]{1,0:T(8,128)(2,1)S(1)}, bf16[128,2048]{1,0:T(8,128)(2,1)}, u32[]{:S(2)}) copy-start(bf16[128,2048]{1,0:T(8,128)(2,1)} %get-tuple-element.134) | copy-start | bytes 1572868
  239.9 11.9 %copy-start = (f32[128,2048]{1,0:T(8,128)S(1)}, f32[128,2048]{1,0:T(8,128)}, u32[]{:S(2)}) copy-start(f32[128,2048]{1,0:T(8,128)} %get-tuple-element.135) | copy-start | bytes 3145732

commit v2 on v1

--- a/solution.py
+++ b/solution.py
@@ -9,7 +9,6 @@
 from jax.sharding import PartitionSpec as P
 
 D = 2048
-HEADS = 16
 HEAD_DIM = 128
 FF = 8192
 RH = 256
@@ -38,10 +37,10 @@
 
 (
     CA, DA, DOWN, DS, EX, FEED, FIRST, GATES, GATHER, GD, GE, GG, GM, GO, GQ, GU, GX, HID, L1,
-    LB, LD, LN, MIXED, MO, MORE, N0, N1, N2, N3, OUT, P0, P1, P2, P3, Q, RF, RT, SA, SD, SL, SQ,
-    SU, T0, T1, T2, T3, TB, TOTAL, U0, U1, U2, U3, UP, V0, V1, V2, V3, WA, WD, WU, Y0, Y1, Y2,
-    Y3,
-) = range(64)
+    LB, LD, LN, LV, MIXED, MO, MORE, N0, N1, N2, N3, OUT, P0, P1, P2, P3, Q, RF, RT, SA, SD, SL,
+    SQ, SU, T0, T1, T2, T3, TB, TOTAL, U0, U1, U2, U3, UP, V0, V1, V2, V3, WA, WD, WU, Y0, Y1,
+    Y2, Y3,
+) = range(65)
 ATTEND = (T0, T1, T2, T3)
 EARLY = (V0, V1, V2, V3)
 UNITS = (U0, U1, U2, U3)
@@ -59,8 +58,8 @@
 FEED_PLAN = (
     GATHER, WU, WU, GATHER, WU, LD, GATHER, WU, WU, V0, WU, GATHER, V1, WU, V3, U1, GATHER, U3,
     N1, N3, GATHER, V2, U2, TOTAL, TOTAL, N2, U0, GE, TOTAL, DS, Y2, MORE, GD, FIRST, N0,
-    GATHER, TOTAL, GU, FIRST, TOTAL, MORE, TOTAL, TOTAL, LB, HID, Y3, Y1, Y0, HID, FIRST, FIRST,
-    MORE, HID,
+    GATHER, TOTAL, GU, FIRST, TOTAL, MORE, TOTAL, TOTAL, LB, HID, LV, Y3, Y1, Y0, HID, FIRST,
+    FIRST, MORE, HID,
 )
 BACKWARD_PLAN = (
     GATHER, UP, LD, GATES, UP, GATHER, GATHER, DOWN, FEED, P0, FEED, GATHER, P3, GATHER, P1,
@@ -89,7 +88,6 @@
 NEAR_Y = [dict(dy=1), dict(dy=-1), dict(dc=1)]
 NARROW_ALL = [dict(dy=a, dc=b) for a in range(SIDE) for b in range(2) if a or b]
 NEAR_XZ = [dict(dx=1), dict(dx=-1), dict(dz=1), dict(dz=-1)]
-LINES_XZ = [dict(dx=a) for a in (1, 2, 3)] + [dict(dz=a) for a in (1, 2, 3)]
 WIDE_ALL = [dict(dx=a, dz=b) for a in range(SIDE) for b in range(SIDE) if a or b]
 
 
@@ -277,25 +275,6 @@
 
 
 GATHER_SMALL_COPIES = 7
-
-
-def gather_call(own, cid, name):
-    rows, cols = own.shape
-
-    def body(net, ins, outs, scr):
-        greet(NEAR_Y)
-        take_turns(gather_narrow(net, ins[0], outs[0]))
-
-    return comm_call(
-        body,
-        [own],
-        [jax.ShapeDtypeStruct((NARROW * rows, cols), own.dtype)],
-        [],
-        cid,
-        GATHER_COPIES,
-        1,
-        name,
-    )[0]
 
 
 def reduce_scratch(rows, cols):
@@ -1045,7 +1024,7 @@
         greet(NARROW_ALL + NEAR_XZ)
         loads.pop(0).wait()
         sums = Pairs(net, None, scr[10:16], far_first=False)
-        stores, dot_copies = [], []
+        stores, dot_copies, gate_grads = [], [], []
 
         def gradient(left, right, to):
             @pl.loop(0, D // strip)
@@ -1122,17 +1101,23 @@
             row = lax.broadcasted_iota(jnp.int32, (TOK, TOK), 0)
             lane = lax.broadcasted_iota(jnp.int32, (TOK, TOK), 1)
             ffn = jnp.sum(jnp.where(row == lane, s[0:1, :], 0.0), axis=-1, keepdims=True)
-            after, attn, gate, gains, slopes, logit_slopes, hidden = held
+            after, attn, gate, gains, slopes = held[:5]
             total = sums.scr[5]
             hat, inverse = normal(after[...])
-            d_gain = jnp.sum(total[...] * hat, axis=0, keepdims=True)
             back = normal_back(hat, inverse, total[...] * gains[1:2, :])
             back = back + dv[span(n * TOK, TOK), :].astype(F32)
-            total[...] = back
             d_attn[...] = (back * gate[:, :1]).astype(BF)
             attn_gate = jnp.sum(back * attn[...], axis=-1, keepdims=True)
             d_hidden[...] = (attn_gate * slopes[0] + ffn * slopes[1]).astype(BF)
-            d_logits = attn_gate * logit_slopes[0] + ffn * logit_slopes[1]
+            attn[...] = back
+            stores.extend([net.keep(attn, after_out), net.keep(d_attn, attn_out)])
+            gate_grads.extend([attn_gate, ffn])
+
+        def fill_vector():
+            after, _, _, _, _, logit_slopes, hidden = held
+            hat, _ = normal(after[...])
+            d_gain = jnp.sum(sums.scr[5][...] * hat, axis=0, keepdims=True)
+            d_logits = gate_grads[0] * logit_slopes[0] + gate_grads[1] * logit_slopes[1]
             d_router = lax.dot_general(
                 d_logits.astype(BF),
                 hidden[...].astype(BF),
@@ -1147,16 +1132,12 @@
                 at = GAIN_ROWS + i * 2 * LEVELS
                 vector[at : at + 2 * LEVELS, :] = d_router[: 2 * LEVELS, i * 128 : (i + 1) * 128]
             own_marks = mv[span(n * TOK, TOK), :]
-            levels = lane.astype(F32)
+            levels = lax.broadcasted_iota(jnp.int32, (TOK, 128), 1).astype(F32)
             picked = jnp.where(levels == own_marks[:, PICK_ATTN : PICK_ATTN + 1], 1.0, 0.0)
             other = own_marks[:, PICK_FFN : PICK_FFN + 1] + float(LEVELS)
             picked = picked + jnp.where(levels == other, 1.0, 0.0)
             vector[SMALL_ROWS : SMALL_ROWS + 1, :] = jnp.sum(picked, axis=0, keepdims=True)
-            pairs = zip(
-                (total, d_attn, vector),
-                (after_out, attn_out, vector_out),
-            )
-            stores.extend([net.keep(a, b) for a, b in pairs])
+            stores.append(net.keep(vector, vector_out))
 
         works = {
             LD: wait_loads,
@@ -1165,6 +1146,7 @@
             GU: up_gradient,
             DS: send_dots,
             LB: second_norm_back,
+            LV: fill_vector,
         }
         for dy in PAIR_ORDER:
             works[EARLY[dy]] = functools.partial(units_of, dy, False)

time: 257 us -> 257 us (level)
  no operation moved by 1% of the time
where the time goes in v2:
time: 257 us; the launch traced here: 253 us
  Pallas kernels  249 us (97%)
    pallas_call x3, Pallas kernels, comm_call(): pl.pallas_call(kernel, out_shape=outs, in_specs=[pl.BlockSpec(memory_spac...  238 us
    pallas_call x1, Pallas kernels, all_steps(): pl.pallas_call(kernel, out_shape=[like(b)] * 3 + [like(b, BF)] + [like(r)...  11.1 us

profile of v2, /device:TPU:1, one launch (start us, length us, event | category | flops | bytes accessed | tf_op | source)
XLA Modules:
  0.0 253.0 jit_solution(18385560484486281508)
XLA Ops:
  0.7 0.7 convert.4
  1.4 0.1 copy.35
  1.5 0.6 pad.5.refs_6_
  2.1 88.0 %attention_forward.1 = (f32[128,2048]{1,0:T(8,128)}, bf16[1024,256]{1,0:T(8,128)(2,1)}, bf16[1024,256]{1,0:T(8,128)(2,1)}, bf16[1024,256]{1,0:T(8,128)(2,1)}, bf...) custom-call(bf16[128,2048]{1,0:T(8,128)(2,1)} %refs_6_.2, ...), custom_call_target="tpu_custom_call" | custom-call | tf_op jit(solution)/shard_map/attention_forward/pallas_call | solution.py:192
  90.1 61.7 %feed_forward.1 = (bf16[1024,2048]{1,0:T(8,128)(2,1)}, bf16[2048,1024]{1,0:T(8,128)(2,1)}, bf16[2,4,64,1024]{3,2,1,0:T(8,128)(2,1)}, f32[128,2048]{1,0:T(8,128)}...) custom-call(bf16[128,2048]{1,0:T(8,128)(2,1)} %get-tuple-element.67.refs_0_, ...), custom_call_target="tpu_custom_call" | custom-call | tf_op jit(solution)/shard_map/feed_forward/pallas_call | solution.py:192
  151.9 88.0 %attention_backward.1 = (f32[128,2048]{1,0:T(8,128)}, bf16[128,2048]{1,0:T(8,128)(2,1)}, bf16[16,24576]{1,0:T(8,128)(2,1)}, bf16[2048,256]{1,0:T(8,128)(2,1)}, f32[64,128]{1,0:T(8,128)}, /*index=5*/f32[8,128]{1,0:T(8,128)}) custom-call(bf16[128,2048]{1,0:T(8,128)(2,1)} %get-tuple-element.80.refs_0_, bf16[1024,2048]{1,0:T(8,128)(2,1)} %get-tuple-element.81.refs_1_, ...), custom_call_target="tpu_custom_call" | custom-call | tf_op jit(solution)/shard_map/attention_backward/pallas_call | solution.py:192
  239.9 0.0 copy-start.1
  239.9 0.0 copy-start
  239.9 11.1 %all_steps.1 = (f32[16,24576]{1,0:T(8,128)}, f32[16,24576]{1,0:T(8,128)}, f32[16,24576]{1,0:T(8,128)}, bf16[16,24576]{1,0:T(8,128)(2,1)}, f32[2048,256]{1,0:T(8,...) custom-call(f32[16,24576]{1,0:T(8,128)} %refs_0_.3, ...), custom_call_target="tpu_custom_call" | custom-call | tf_op jit(solution)/shard_map/all_steps/pallas_call | solution.py:1617
  251.0 0.0 copy-done.1
  251.0 0.8 copy.38
  251.8 0.0 copy-done
  251.8 1.0 copy.39
Async XLA Ops:
  239.9 11.1 %copy-start.1 = (bf16[128,2048]{1,0:T(8,128)(2,1)S(1)}, bf16[128,2048]{1,0:T(8,128)(2,1)}, u32[]{:S(2)}) copy-start(bf16[128,2048]{1,0:T(8,128)(2,1)} %get-tuple-element.134) | copy-start | bytes 1572868
  239.9 11.9 %copy-start = (f32[128,2048]{1,0:T(8,128)S(1)}, f32[128,2048]{1,0:T(8,128)}, u32[]{:S(2)}) copy-start(f32[128,2048]{1,0:T(8,128)} %get-tuple-element.135) | copy-start | bytes 3145732
